TPU v7x, 512 devices: a whole 4x8x8 slice. The times are simulated.
512 devices in a mesh: dp: 32 (over z, x_lo, core), seq: 16 (over y, x_hi).
Axes of the slice: x: 4 (x_hi: 2, x_lo: 2; x = x_hi * 2 + x_lo), y: 8, z: 8, core: 2. Of those that a mesh axis runs over, the one named last changes fastest.
Arguments:
- query_saved: bfloat16 [32, 64, 32, 2048], P('dp', 'seq'), may hold values from -24 to 24
- key_saved: bfloat16 [32, 64, 32, 2048], P('dp', 'seq'), may hold values from -24 to 24
- value_saved: bfloat16 [32, 64, 32, 2048], P('dp', 'seq'), may hold values from -6 to 6
- grad_block: bfloat16 [32, 64, 32, 2048], P('dp', 'seq'), may hold values from -6 to 6
- out_weight: bfloat16 [2048, 2048], P('seq', 'dp'), may hold values from -0.125 to 0.125
Outputs:
- grad_query: bfloat16 [32, 64, 32, 2048], P('dp', 'seq')
- grad_key: bfloat16 [32, 64, 32, 2048], P('dp', 'seq')
- grad_value: bfloat16 [32, 64, 32, 2048], P('dp', 'seq')
All inputs are finite; a program needn't handle non-finite values.
Results may differ from a plain program's by a relative error of at most 0.012.
The roundings to bfloat16 on the way count: a program that leaves them out, or rounds other values in their place, can miss the bound.
Values may be sent and summed in bfloat16 or wider, within the bound.
A program may use at most 64 MiB of HBM per device.

v0:
```python
import math

import jax
import jax.numpy as jnp
from jax import lax
from jax.sharding import PartitionSpec as P

HD = 128


def split_heads(tensor):
    return tensor.reshape(tensor.shape[1], tensor.shape[2], tensor.shape[3] // HD, HD)


def backward_local(query_in, key_in, value_in, grad_in):
    outer = query_in.shape
    query_in = split_heads(query_in)
    key_in = split_heads(key_in)
    value_in = split_heads(value_in)
    grad_in = split_heads(grad_in)
    inv_root = 1.0 / math.sqrt(HD)
    frames_all = query_in.shape[0]
    scores = (
        jnp.einsum("fxhd,gxhd->xhfg", query_in, key_in, preferred_element_type=jnp.float32)
        * inv_root
    )
    later = lax.broadcasted_iota(jnp.int32, (frames_all, frames_all), 0)
    earlier = lax.broadcasted_iota(jnp.int32, (frames_all, frames_all), 1)
    scores = jnp.where(later >= earlier, scores, -1e30)
    row_max = jnp.max(scores, axis=-1, keepdims=True)
    exponent = jnp.exp(scores - row_max)
    probable = exponent / jnp.sum(exponent, axis=-1, keepdims=True)
    probs_low = probable.astype(jnp.bfloat16)
    attended = jnp.einsum(
        "xhfg,gxhd->fxhd", probs_low, value_in, preferred_element_type=jnp.float32
    )
    row_delta = jnp.sum(grad_in.astype(jnp.float32) * attended, axis=-1)
    grad_value = jnp.einsum(
        "xhfg,fxhd->gxhd", probs_low, grad_in, preferred_element_type=jnp.float32
    ).astype(jnp.bfloat16)
    grad_prob = jnp.einsum("fxhd,gxhd->xhfg", grad_in, value_in, preferred_element_type=jnp.float32)
    grad_score = (
        probable * (grad_prob - jnp.transpose(row_delta, (1, 2, 0))[..., None]) * inv_root
    ).astype(jnp.bfloat16)
    grad_query = jnp.einsum(
        "xhfg,gxhd->fxhd", grad_score, key_in, preferred_element_type=jnp.float32
    ).astype(jnp.bfloat16)
    grad_key = jnp.einsum(
        "xhfg,fxhd->gxhd", grad_score, query_in, preferred_element_type=jnp.float32
    ).astype(jnp.bfloat16)
    return (grad_query.reshape(outer), grad_key.reshape(outer), grad_value.reshape(outer))


def body(query_saved, key_saved, value_saved, grad_block, out_weight):
    columns = lax.all_gather(out_weight, "dp", axis=1, tiled=True)
    flat_grad = grad_block.reshape(-1, grad_block.shape[3])
    grad_attn = jnp.einsum(
        "td,rd->tr",
        flat_grad,
        lax.all_gather(columns, "seq", axis=0, tiled=True),
        preferred_element_type=jnp.float32,
    )
    grad_attn = grad_attn.astype(jnp.bfloat16).reshape(grad_block.shape)
    query_moved, key_moved, value_moved, grad_moved = (
        lax.all_to_all(query_saved, "seq", split_axis=2, concat_axis=1, tiled=True),
        lax.all_to_all(key_saved, "seq", split_axis=2, concat_axis=1, tiled=True),
        lax.all_to_all(value_saved, "seq", split_axis=2, concat_axis=1, tiled=True),
        lax.all_to_all(grad_attn, "seq", split_axis=2, concat_axis=1, tiled=True),
    )
    results = backward_local(query_moved, key_moved, value_moved, grad_moved)
    grad_query, grad_key, grad_value = (
        lax.all_to_all(results[0], "seq", split_axis=1, concat_axis=2, tiled=True),
        lax.all_to_all(results[1], "seq", split_axis=1, concat_axis=2, tiled=True),
        lax.all_to_all(results[2], "seq", split_axis=1, concat_axis=2, tiled=True),
    )
    return (grad_query, grad_key, grad_value)


def solution(mesh):
    in_specs = (
        P("dp", "seq", None, None),
        P("dp", "seq", None, None),
        P("dp", "seq", None, None),
        P("dp", "seq", None, None),
        P("seq", "dp"),
    )
    out_specs = (P("dp", "seq", None, None), P("dp", "seq", None, None), P("dp", "seq", None, None))
    return jax.shard_map(body, mesh=mesh, in_specs=in_specs, out_specs=out_specs, check_vma=False)
```

profile of v0, /device:TPU:1, one launch (start us, length us, event | category | flops | bytes accessed | tf_op | source)
XLA Modules:
  0.0 315.0 jit_solution(11145494248644493565)
XLA Ops:
  7.2 46.1 %all_gather.6 = bf16[128,2048]{0,1:T(8,128)(2,1)} all-gather(bf16[128,64]{0,1:T(8,128)(2,1)} %param.9), channel_id=1, replica_groups=mesh['dp'=32,'seq'=16] {'dp'}, dimensions={1}, use_global_device_ids=true | all-gather | bytes 540672 | tf_op jit(solution)/shard_map/all_gather | solution.py:55
  53.4 2.2 copy.69
  55.6 9.1 %all-to-all-start.3 = ((bf16[1,4,32,2048]{3,1,0,2:T(4,128)(2,1)}), bf16[1,4,32,2048]{3,1,0,2:T(4,128)(2,1)S(1)}, u32[]{:S(2)}, u32[]{:S(2)}) async-start(bf16[1,4,32,2048]{3,1,0,2:T(4,128)(2,1)} %copy.69), calls=%async_computation.3 | async-start | bytes 1048576 | tf_op jit(solution)/shard_map/all_to_all | solution.py:67
  64.7 2.3 copy.63
  67.0 20.6 %all-to-all-done.3 = bf16[1,4,32,2048]{3,1,0,2:T(4,128)(2,1)S(1)} async-done(((bf16[1,4,32,2048]{3,1,0,2:T(4,128)(2,1)}), bf16[1,4,32,2048]{3,1,0,2:T(4,128)(2,1)S(1)}, u32[]{:S(2)}, u32[]{:S(2)}) %all-to-all-start.3) | async-done | bytes 524320 | tf_op jit(solution)/shard_map/all_to_all | solution.py:67
  87.6 3.6 %all-to-all-start.1 = ((bf16[1,4,32,2048]{3,1,0,2:T(4,128)(2,1)}), bf16[1,4,32,2048]{3,1,0,2:T(4,128)(2,1)S(1)}, u32[]{:S(2)}, u32[]{:S(2)}) async-start(bf16[1,4,32,2048]{3,1,0,2:T(4,128)(2,1)} %copy.63), calls=%async_computation.1 | async-start | bytes 1048576 | tf_op jit(solution)/shard_map/all_to_all | solution.py:66
  91.1 2.3 copy.61
  93.4 19.6 %all-to-all-done.1 = bf16[1,4,32,2048]{3,1,0,2:T(4,128)(2,1)S(1)} async-done(((bf16[1,4,32,2048]{3,1,0,2:T(4,128)(2,1)}), bf16[1,4,32,2048]{3,1,0,2:T(4,128)(2,1)S(1)}, u32[]{:S(2)}, u32[]{:S(2)}) %all-to-all-start.1) | async-done | bytes 524320 | tf_op jit(solution)/shard_map/all_to_all | solution.py:66
  113.0 3.6 %all-to-all-start = ((bf16[1,4,32,2048]{3,1,0,2:T(4,128)(2,1)}), bf16[1,4,32,2048]{3,1,0,2:T(4,128)(2,1)S(1)}, u32[]{:S(2)}, u32[]{:S(2)}) async-start(bf16[1,4,32,2048]{3,1,0,2:T(4,128)(2,1)} %copy.61), calls=%async_computation | async-start | bytes 1048576 | tf_op jit(solution)/shard_map/all_to_all | solution.py:65
  116.6 105.0 %all-gather.2.cloned.1.call-done = bf16[2048,2048]{0,1:T(8,128)(2,1)} async-done(((bf16[128,2048]{0,1:T(8,128)(2,1)}), bf16[2048,2048]{0,1:T(8,128)(2,1)}) %all-gather.2.cloned.1.call-update) | async-done | bytes 8388624 | tf_op jit(solution)/shard_map/all_gather | solution.py:60
  221.5 4.6 %convolution_convert_fusion = bf16[128,2048]{1,0:T(8,128)(2,1)S(1)} fusion(bf16[128,2048]{1,0:T(8,128)(2,1)S(1)} %bitcast.55, bf16[2048,2048]{0,1:T(8,128)(2,1)} %all-gather.2.cloned.1.call-done), kind=kOutput, calls=%fused_computation.1 | convolution fusion | flops 1074003968 | bytes 9437184 | tf_op jit(solution)/shard_map/td,rd->tr/dot_general | solution.py:57
  226.2 1.2 copy.67
  227.4 3.6 %all-to-all-start.2 = ((bf16[1,4,32,2048]{3,1,0,2:T(4,128)(2,1)}), bf16[1,4,32,2048]{3,1,0,2:T(4,128)(2,1)S(1)}, u32[]{:S(2)}, u32[]{:S(2)}) async-start(bf16[1,4,32,2048]{3,1,0,2:T(4,128)(2,1)} %copy.67), calls=%async_computation.2 | async-start | bytes 1048576 | tf_op jit(solution)/shard_map/all_to_all | solution.py:68
  231.0 0.5 copy.122
  231.5 1.1 reshape.45
  232.7 0.5 copy.123
  233.2 0.3 reshape.41
  233.6 0.5 copy.124
  234.1 0.3 reshape.40
  234.4 0.5 fusion.6
  235.0 1.0 copy-done.1
  236.0 1.3 fusion.23
  237.2 8.4 %all-to-all-done.2 = bf16[1,4,32,2048]{3,1,0,2:T(4,128)(2,1)S(1)} async-done(((bf16[1,4,32,2048]{3,1,0,2:T(4,128)(2,1)}), bf16[1,4,32,2048]{3,1,0,2:T(4,128)(2,1)S(1)}, u32[]{:S(2)}, u32[]{:S(2)}) %all-to-all-start.2) | async-done | bytes 524320 | tf_op jit(solution)/shard_map/all_to_all | solution.py:68
  245.6 0.5 copy.68
  246.1 0.3 reshape.44
  246.5 2.4 fusion.8
  248.9 2.0 fusion.7
  250.9 0.4 fusion.9
  251.2 0.3 copy.96
  251.6 0.9 reshape.49
  252.5 4.4 %all-to-all-start.4 = ((bf16[1,64,2,2048]{3,2,0,1:T(2,128)(2,1)}), bf16[1,64,2,2048]{3,2,0,1:T(2,128)(2,1)S(1)}, u32[]{:S(2)}, u32[]{:S(2)}) async-start(bf16[1,64,2,2048]{3,2,0,1:T(2,128)(2,1)} %reshape.49), calls=%async_computation.4 | async-start | bytes 1048576 | tf_op jit(solution)/shard_map/all_to_all | solution.py:72
  256.9 0.3 fusion.10
  257.2 0.3 copy.97
  257.6 0.9 reshape.50
  258.5 11.8 %all-to-all-done.4 = bf16[1,64,2,2048]{3,2,0,1:T(2,128)(2,1)S(1)} async-done(((bf16[1,64,2,2048]{3,2,0,1:T(2,128)(2,1)}), bf16[1,64,2,2048]{3,2,0,1:T(2,128)(2,1)S(1)}, u32[]{:S(2)}, u32[]{:S(2)}) %all-to-all-start.4) | async-done | bytes 524320 | tf_op jit(solution)/shard_map/all_to_all | solution.py:72
  270.3 5.0 %all-to-all-start.5 = ((bf16[1,64,2,2048]{3,2,0,1:T(2,128)(2,1)}), bf16[1,64,2,2048]{3,2,0,1:T(2,128)(2,1)S(1)}, u32[]{:S(2)}, u32[]{:S(2)}) async-start(bf16[1,64,2,2048]{3,2,0,1:T(2,128)(2,1)} %reshape.50), calls=%async_computation.5 | async-start | bytes 1048576 | tf_op jit(solution)/shard_map/all_to_all | solution.py:73
  275.3 2.1 fusion.11
  277.4 0.3 copy.98
  277.7 0.9 reshape.51
  278.7 10.0 %all-to-all-done.5 = bf16[1,64,2,2048]{3,2,0,1:T(2,128)(2,1)S(1)} async-done(((bf16[1,64,2,2048]{3,2,0,1:T(2,128)(2,1)}), bf16[1,64,2,2048]{3,2,0,1:T(2,128)(2,1)S(1)}, u32[]{:S(2)}, u32[]{:S(2)}) %all-to-all-start.5) | async-done | bytes 524320 | tf_op jit(solution)/shard_map/all_to_all | solution.py:73
  288.7 4.5 %all-to-all-start.6 = ((bf16[1,64,2,2048]{3,2,0,1:T(2,128)(2,1)}), bf16[1,64,2,2048]{3,2,0,1:T(2,128)(2,1)S(1)}, u32[]{:S(2)}, u32[]{:S(2)}) async-start(bf16[1,64,2,2048]{3,2,0,1:T(2,128)(2,1)} %reshape.51), calls=%async_computation.6 | async-start | bytes 1048576 | tf_op jit(solution)/shard_map/all_to_all | solution.py:74
  293.2 0.3 copy.81
  293.5 1.1 copy.90
  294.6 0.3 copy.85
  294.9 1.1 copy.91
  296.0 10.8 %all-to-all-done.6 = bf16[1,64,2,2048]{3,2,0,1:T(2,128)(2,1)S(1)} async-done(((bf16[1,64,2,2048]{3,2,0,1:T(2,128)(2,1)}), bf16[1,64,2,2048]{3,2,0,1:T(2,128)(2,1)S(1)}, u32[]{:S(2)}, u32[]{:S(2)}) %all-to-all-start.6) | async-done | bytes 524320 | tf_op jit(solution)/shard_map/all_to_all | solution.py:74
  306.8 0.3 copy.89
  307.1 1.1 copy.92
  (7 shorter events, 0.1 us)
Async XLA Ops:
  7.2 214.4 %copy-start = (bf16[1,4,32,2048]{3,2,1,0:T(8,128)(2,1)S(1)}, bf16[1,4,32,2048]{3,2,1,0:T(8,128)(2,1)}, u32[]{:S(2)}) copy-start(bf16[1,4,32,2048]{3,2,1,0:T(8,128)(2,1)} %param.8) | copy-start | bytes 1572868
  7.2 214.4 %all-gather.2.cloned.1.call-start = ((), (), s32[]{:S(2)}) async-start(), calls=%async_computation.7 | async-start | bytes 8912896 | tf_op jit(solution)/shard_map/all_gather | solution.py:60
  55.6 31.9 %all-to-all-start.3 = ((bf16[1,4,32,2048]{3,1,0,2:T(4,128)(2,1)}), bf16[1,4,32,2048]{3,1,0,2:T(4,128)(2,1)S(1)}, u32[]{:S(2)}, u32[]{:S(2)}) async-start(bf16[1,4,32,2048]{3,1,0,2:T(4,128)(2,1)} %copy.69), calls=%async_computation.3 | async-start | bytes 1048576 | tf_op jit(solution)/shard_map/all_to_all | solution.py:67
  87.6 25.4 %all-to-all-start.1 = ((bf16[1,4,32,2048]{3,1,0,2:T(4,128)(2,1)}), bf16[1,4,32,2048]{3,1,0,2:T(4,128)(2,1)S(1)}, u32[]{:S(2)}, u32[]{:S(2)}) async-start(bf16[1,4,32,2048]{3,1,0,2:T(4,128)(2,1)} %copy.63), calls=%async_computation.1 | async-start | bytes 1048576 | tf_op jit(solution)/shard_map/all_to_all | solution.py:66
  113.0 114.4 %all-to-all-start = ((bf16[1,4,32,2048]{3,1,0,2:T(4,128)(2,1)}), bf16[1,4,32,2048]{3,1,0,2:T(4,128)(2,1)S(1)}, u32[]{:S(2)}, u32[]{:S(2)}) async-start(bf16[1,4,32,2048]{3,1,0,2:T(4,128)(2,1)} %copy.61), calls=%async_computation | async-start | bytes 1048576 | tf_op jit(solution)/shard_map/all_to_all | solution.py:65
  227.4 18.2 %all-to-all-start.2 = ((bf16[1,4,32,2048]{3,1,0,2:T(4,128)(2,1)}), bf16[1,4,32,2048]{3,1,0,2:T(4,128)(2,1)S(1)}, u32[]{:S(2)}, u32[]{:S(2)}) async-start(bf16[1,4,32,2048]{3,1,0,2:T(4,128)(2,1)} %copy.67), calls=%async_computation.2 | async-start | bytes 1048576 | tf_op jit(solution)/shard_map/all_to_all | solution.py:68
  235.0 1.0 copy-start.1
  252.5 17.8 %all-to-all-start.4 = ((bf16[1,64,2,2048]{3,2,0,1:T(2,128)(2,1)}), bf16[1,64,2,2048]{3,2,0,1:T(2,128)(2,1)S(1)}, u32[]{:S(2)}, u32[]{:S(2)}) async-start(bf16[1,64,2,2048]{3,2,0,1:T(2,128)(2,1)} %reshape.49), calls=%async_computation.4 | async-start | bytes 1048576 | tf_op jit(solution)/shard_map/all_to_all | solution.py:72
  270.3 18.4 %all-to-all-start.5 = ((bf16[1,64,2,2048]{3,2,0,1:T(2,128)(2,1)}), bf16[1,64,2,2048]{3,2,0,1:T(2,128)(2,1)S(1)}, u32[]{:S(2)}, u32[]{:S(2)}) async-start(bf16[1,64,2,2048]{3,2,0,1:T(2,128)(2,1)} %reshape.50), calls=%async_computation.5 | async-start | bytes 1048576 | tf_op jit(solution)/shard_map/all_to_all | solution.py:73
  288.7 18.1 %all-to-all-start.6 = ((bf16[1,64,2,2048]{3,2,0,1:T(2,128)(2,1)}), bf16[1,64,2,2048]{3,2,0,1:T(2,128)(2,1)S(1)}, u32[]{:S(2)}, u32[]{:S(2)}) async-start(bf16[1,64,2,2048]{3,2,0,1:T(2,128)(2,1)} %reshape.51), calls=%async_computation.6 | async-start | bytes 1048576 | tf_op jit(solution)/shard_map/all_to_all | solution.py:74
Sparse Core Ops, SparseCore 0:
  53.5 168.0 all-gather.1
where the time goes:
time: 321 us; the launch traced here: 315 us
  waiting for transfers between devices  186 us (58%)
  blocking collectives  46.1 us (14%)
  starting transfers between devices  33.8 us (11%)
  local copies, waits for them, and re-layouts  21.1 us (7%)
  between operations  14.2 us (4%)
  matrix products  12.3 us (4%)
    all_gather x1, waiting for transfers between devices, body(): lax.all_gather(columns, 'seq', axis=0, tiled=True)  105 us
    all_gather x1, blocking collectives, body(): columns = lax.all_gather(out_weight, 'dp', axis=1, tiled=True)  46.1 us
    all_to_all x1, waiting for transfers between devices, body(): lax.all_to_all(value_saved, 'seq', split_axis=2, concat_axis=1, tiled=True)  20.6 us
    all_to_all x1, waiting for transfers between devices, body(): lax.all_to_all(key_saved, 'seq', split_axis=2, concat_axis=1, tiled=True)  19.6 us
    all_to_all x1, waiting for transfers between devices, body(): lax.all_to_all(results[0], 'seq', split_axis=1, concat_axis=2, tiled=True)  11.8 us
    unnamed x10, local copies, waits for them, and re-layouts  11 us
    all_to_all x1, waiting for transfers between devices, body(): lax.all_to_all(results[2], 'seq', split_axis=1, concat_axis=2, tiled=True)  10.8 us
    all_to_all x1, waiting for transfers between devices, body(): lax.all_to_all(results[1], 'seq', split_axis=1, concat_axis=2, tiled=True)  10 us
  transfers between devices with their start and end apart: 8, of which 7 were waited for; matrix products, arithmetic and copies ran while one was open for 8% of the time, Pallas kernels for 0%

commit v1 on v0

v1 whole, which is shorter than its diff:
```python
import functools
import math

import jax
import jax.numpy as jnp
from jax import lax
from jax.experimental import pallas as pl
from jax.experimental.pallas import tpu as pltpu
from jax.sharding import PartitionSpec as P

HD = 128
F32 = jnp.float32
BF16 = jnp.bfloat16
MESH = pl.DeviceIdType.MESH
NT = (((1,), (1,)), ((), ()))
TN = (((0,), (0,)), ((), ()))
NN = (((1,), (0,)), ((), ()))


def dot(a, b, dims):
    return lax.dot_general(a, b, dims, preferred_element_type=F32)


def kernel(
    q, k, v, g, w, oq, ok, ov,
    rq, rk, rv, rg, gbuf, wt, ga, x32, qt, kt, vt, gt, pt, o32, so,
    in_send, in_recv, w_send, w_recv, z_send, z_recv, g_send, g_recv, ga_send, ga_recv, o_send, o_recv,
):
    dp, s = lax.axis_index("dp"), lax.axis_index("seq")
    z, u = lax.div(dp, 4), lax.rem(dp, 4)
    own_class = lax.div(s, 4)
    base = z * 4
    own = own_class == u
    inv_root = 1.0 / math.sqrt(HD)

    def ring(i, n):
        return lax.rem(i + n, n)

    up, down = ring(z + 1, 8) * 4 + u, ring(z - 1, 8) * 4 + u
    sibling = base + (u + 1 - 2 * lax.rem(u, 2))
    across = base + lax.rem(u + 2, 4)

    barrier = pltpu.get_barrier_semaphore()

    def greet(d, e):
        pl.semaphore_signal(barrier, inc=1, device_id=(d, e), device_id_type=MESH)

    def greet_seq(i, _):
        greet(dp, lax.rem(s + i, 16))
        return 0

    lax.fori_loop(1, 16, greet_seq, 0)

    def greet_group(i, _):
        t = lax.rem(s + i, 16)

        @pl.when(jnp.logical_or(base + lax.div(t, 4) != dp, 4 * u + lax.rem(t, 4) != s))
        def _():
            greet(base + lax.div(t, 4), 4 * u + lax.rem(t, 4))

        @pl.when(jnp.logical_or(own_class != u, t != s))
        def _():
            greet(base + own_class, t)

        return 0

    lax.fori_loop(0, 16, greet_group, 0)
    for d in (up, down, sibling, across):
        greet(d, s)
    pl.semaphore_wait(barrier, 51 - 2 * own.astype(jnp.int32))

    def w_rows():
        return wt.at[pl.ds(pl.multiple_of(dp * 64, 64), 64), pl.ds(pl.multiple_of(lax.rem(s, 4) * HD, HD), HD)]

    def w_copy(t):
        return pltpu.make_async_remote_copy(
            src_ref=w, dst_ref=w_rows(), send_sem=w_send, recv_sem=w_recv,
            device_id=(base + own_class, t), device_id_type=MESH)

    def w_go(i, _):
        t = lax.rem(s + i, 16)
        mine = jnp.logical_and(own, t == s)

        @pl.when(mine)
        def _():
            pltpu.make_async_copy(w, w_rows(), w_recv).start()

        @pl.when(jnp.logical_not(mine))
        def _():
            w_copy(t).start()

        return 0

    lax.fori_loop(0, 16, w_go, 0)

    pltpu.make_async_copy(g.at[0], gbuf.at[u], g_recv.at[0]).start()

    def g_copy(n, src, slot, d):
        return pltpu.make_async_remote_copy(
            src_ref=src, dst_ref=gbuf.at[slot], send_sem=g_send.at[n], recv_sem=g_recv.at[n],
            device_id=(d, s), device_id_type=MESH)

    to_across = g_copy(1, g.at[0], u, across)
    to_sibling = g_copy(2, g.at[0], u, sibling)
    across_slot = lax.rem(u + 2, 4)
    onward = g_copy(3, gbuf.at[across_slot], across_slot, sibling)
    to_across.start()
    to_sibling.start()

    pairs = ((q, rq), (k, rk), (v, rv))

    def lanes(h):
        return pl.ds(pl.multiple_of(h * HD, HD), HD)

    for n, (src, dst) in enumerate(pairs):
        pltpu.make_async_copy(src.at[0, :, :, lanes(s)], dst.at[s], in_recv.at[n]).start()

        def in_go(i, _, src=src, dst=dst, n=n):
            t = lax.rem(s + i, 16)
            pltpu.make_async_remote_copy(
                src_ref=src.at[0, :, :, lanes(t)], dst_ref=dst.at[s], send_sem=in_send.at[n], recv_sem=in_recv.at[n],
                device_id=(dp, t), device_id_type=MESH).start()
            return 0

        lax.fori_loop(1, 16, in_go, 0)

    def z_copy(way, h, step):
        slab = ring(z - step, 8) if way == 0 else ring(z + step, 8)
        rows = wt.at[pl.ds(pl.multiple_of(slab * 256 + h * 128, 128), 128)]
        return pltpu.make_async_remote_copy(
            src_ref=rows, dst_ref=rows, send_sem=z_send.at[way, h, step], recv_sem=z_recv.at[way, h, step],
            device_id=(up if way == 0 else down, s), device_id_type=MESH)

    def z_arrived(way, h, step):
        slab = ring(z - step - 1, 8) if way == 0 else ring(z + step + 1, 8)
        rows = wt.at[pl.ds(pl.multiple_of(slab * 256 + h * 128, 128), 128)]
        pltpu.make_async_remote_copy(
            src_ref=rows, dst_ref=rows, send_sem=z_send.at[way, h, step], recv_sem=z_recv.at[way, h, step],
            device_id=(up if way == 0 else down, s), device_id_type=MESH).wait_recv()

    hops = [(step, way, h) for step in range(4) for h in range(2) for way in range(2) if step < 3 or way == h]
    mine = wt.at[pl.ds(pl.multiple_of(z * 256, 256), 256)]
    pltpu.make_async_copy(mine, mine, w_recv).wait()
    for step, way, h in hops:
        if step:
            z_arrived(way, h, step - 1)
        z_copy(way, h, step).start()
        if (step, way, h) == (1, 1, 1):
            to_across.wait_recv()
            onward.start()
    for way, h in ((0, 1), (1, 0)):
        z_arrived(way, h, 2)
    for way in range(2):
        z_arrived(way, way, 3)

    pltpu.make_async_copy(g.at[0], gbuf.at[u], g_recv.at[0]).wait()
    to_sibling.wait_recv()
    onward.wait_recv()

    for half in range(2):
        acc = dot(gbuf[...].reshape(512, 2048), wt[:, half * 256 : half * 256 + 256], NN)
        acc = acc.astype(BF16)
        for j in range(2):
            ga[2 * half + j] = acc[:, j * HD : (j + 1) * HD].reshape(4, 4, 32, HD)

    def patches(c):
        return pl.ds(c * 16, 16)

    def ga_copy(c, t):
        b, j = lax.div(t, 4), lax.rem(t, 4)
        return pltpu.make_async_remote_copy(
            src_ref=ga.at[j, b, :, patches(c)], dst_ref=rg.at[s, :, patches(c)],
            send_sem=ga_send.at[c], recv_sem=ga_recv.at[c],
            device_id=(base + b, 4 * u + j), device_id_type=MESH)

    for c in range(2):

        def ga_go(i, _, c=c):
            t = lax.rem(s + i, 16)
            b, j = lax.div(t, 4), lax.rem(t, 4)
            mine = jnp.logical_and(b == u, 4 * u + j == s)

            @pl.when(mine)
            def _():
                pltpu.make_async_copy(ga.at[j, b, :, patches(c)], rg.at[s, :, patches(c)], ga_recv.at[c]).start()

            @pl.when(jnp.logical_not(mine))
            def _():
                ga_copy(c, t).start()

            return 0

        lax.fori_loop(0, 16, ga_go, 0)

    key_at = lax.broadcasted_iota(jnp.int32, (128, 128), 0)
    query_at = lax.broadcasted_iota(jnp.int32, (128, 128), 1)
    seen = jnp.logical_and(query_at >= key_at, (query_at >= 64) == (key_at >= 64))

    def widen(src):
        def step(i, _):
            x32[pl.ds(pl.multiple_of(i * 128, 128), 128)] = src[i].reshape(128, HD).astype(F32)
            return 0

        lax.fori_loop(0, 16, step, 0)

    def pair_of(p):
        a = x32[pl.ds(2 * p, 64, stride=32), :]
        b = x32[pl.ds(2 * p + 1, 64, stride=32), :]
        return jnp.concatenate([a, b], axis=0).astype(BF16)

    for n, (dst, out) in enumerate(((rq, qt), (rk, kt), (rv, vt))):
        pltpu.make_async_copy(dst, dst, in_recv.at[n]).wait()
        widen(dst)

        def regroup(p, _, out=out):
            out[p] = pair_of(p)
            return 0

        lax.fori_loop(0, 16, regroup, 0)

    def soft(p, _):
        scores = jnp.where(seen, dot(kt[p], qt[p], NT) * inv_root, -1e30)
        e = jnp.exp(scores - jnp.max(scores, axis=0, keepdims=True))
        pt[p] = e / jnp.sum(e, axis=0, keepdims=True)
        return 0

    lax.fori_loop(0, 16, soft, 0)

    outs = (oq, ok, ov)

    def out_copy(n, c, d):
        return pltpu.make_async_remote_copy(
            src_ref=so.at[n, d, :, patches(c)], dst_ref=outs[n].at[0, :, patches(c), lanes(s)],
            send_sem=o_send.at[n], recv_sem=o_recv.at[n],
            device_id=(dp, d), device_id_type=MESH)

    for c in range(2):
        part = rg.at[:, :, patches(c)]
        pltpu.make_async_copy(part, part, ga_recv.at[c]).wait()

        def widen_g(i, _, c=c):
            for f in range(4):
                x32[pl.ds(pl.multiple_of(i * 128 + f * 32 + c * 16, 16), 16)] = rg[i, f, c * 16 : c * 16 + 16].astype(F32)
            return 0

        lax.fori_loop(0, 16, widen_g, 0)

        def grads(p, _):
            gp, vp, prob = pair_of(p), vt[p], pt[p]
            low = prob.astype(BF16)
            grad_prob = dot(vp, gp, NT)
            delta = jnp.sum(low.astype(F32) * grad_prob, axis=0, keepdims=True)
            ds = (prob * (grad_prob - delta) * inv_root).astype(BF16)
            for n, val in ((2, dot(low, gp, NN)), (1, dot(ds, qt[p], NN)), (0, dot(ds, kt[p], TN))):
                o32[n, pl.ds(2 * p, 64, stride=32), :] = val[:64]
                o32[n, pl.ds(2 * p + 1, 64, stride=32), :] = val[64:]
            return 0

        lax.fori_loop(c * 8, c * 8 + 8, grads, 0)

        for n in range(3):

            def narrow(i, _, n=n, c=c):
                for f in range(4):
                    rows = pl.ds(pl.multiple_of(i * 128 + f * 32 + c * 16, 16), 16)
                    so[n, i, f, c * 16 : c * 16 + 16] = o32[n, rows, :].astype(BF16)
                return 0

            lax.fori_loop(0, 16, narrow, 0)
            pltpu.make_async_copy(
                so.at[n, s, :, patches(c)], outs[n].at[0, :, patches(c), lanes(s)], o_recv.at[n]).start()

            def out_go(i, _, n=n, c=c):
                out_copy(n, c, lax.rem(s + i, 16)).start()
                return 0

            lax.fori_loop(1, 16, out_go, 0)

    for n, (src, dst) in enumerate(pairs):
        part = src.at[0, :, :, pl.ds(0, 15 * HD)]
        pltpu.make_async_copy(part, part, in_send.at[n]).wait()
    for step, way, h in hops:
        z_copy(way, h, step).wait_send()
    for copy in (to_across, to_sibling, onward):
        copy.wait_send()

    def drain(ref, sem):
        pltpu.make_async_copy(ref, ref, sem).wait()

    @pl.when(own)
    def _():
        drain(wt.at[pl.ds(0, 240)], w_send)
        for c in range(2):
            drain(rg.at[pl.ds(0, 15), :, patches(c)], ga_send.at[c])

    @pl.when(jnp.logical_not(own))
    def _():
        drain(wt.at[pl.ds(0, 256)], w_send)
        for c in range(2):
            drain(rg.at[:, :, patches(c)], ga_send.at[c])

    for n in range(3):
        drain(so.at[n, pl.ds(0, 15)], o_send.at[n])
        drain(outs[n], o_recv.at[n])


def body(query_saved, key_saved, value_saved, grad_block, out_weight):
    shape = jax.ShapeDtypeStruct(query_saved.shape, BF16)
    anywhere = pl.BlockSpec(memory_space=pl.ANY)
    dma = pltpu.SemaphoreType.DMA
    return pl.pallas_call(
        kernel,
        out_shape=(shape, shape, shape),
        in_specs=[anywhere] * 5,
        out_specs=(anywhere,) * 3,
        scratch_shapes=[
            *[pltpu.VMEM((16, 4, 32, HD), BF16)] * 4,
            pltpu.VMEM((4, 4, 32, 2048), BF16),
            pltpu.VMEM((2048, 512), BF16),
            pltpu.VMEM((4, 4, 4, 32, HD), BF16),
            pltpu.VMEM((2048, HD), F32),
            *[pltpu.VMEM((16, 128, HD), BF16)] * 4,
            pltpu.VMEM((16, 128, 128), F32),
            pltpu.VMEM((3, 2048, HD), F32),
            pltpu.VMEM((3, 16, 4, 32, HD), BF16),
            dma((3,)), dma((3,)),
            dma, dma,
            dma((2, 2, 4)), dma((2, 2, 4)),
            dma((4,)), dma((4,)),
            dma((2,)), dma((2,)),
            dma((3,)), dma((3,)),
        ],
        compiler_params=pltpu.CompilerParams(
            collective_id=0, has_side_effects=True, vmem_limit_bytes=48 * 1024 * 1024),
    )(query_saved, key_saved, value_saved, grad_block, out_weight.T)


def solution(mesh):
    spec = P("dp", "seq", None, None)
    return jax.shard_map(
        body, mesh=mesh, in_specs=(spec, spec, spec, spec, P("seq", "dp")), out_specs=(spec, spec, spec), check_vma=False)
```

time: 321 us -> 125 us (0.39); the launches traced: 315 us -> 125 us
  waiting for transfers between devices: 186 us -> 0 us
  Pallas kernels: 0 us -> 117 us
  blocking collectives: 46.1 us -> 0 us
  starting transfers between devices: 33.8 us -> 0 us
  local copies, waits for them, and re-layouts: 21.1 us -> 7.26 us
  between operations: 14.2 us -> 0.65 us
  matrix products: 12.3 us -> 0 us
    pallas_call x0 -> x1, Pallas kernels: none -> 117 us  [body(): pl.pallas_call(kernel, out_shape=(shape, shape, shape), in_specs=[anywher...]
    all_gather x1 -> x0, waiting for transfers between devices: 105 us -> none  [body(): lax.all_gather(columns, 'seq', axis=0, tiled=True)]
    all_to_all x7 -> x0, waiting for transfers between devices: 81.2 us -> none  [the longest x1 20.6 us: body(): lax.all_to_all(value_saved, 'seq', split_axis=2, concat_axis=1, tiled=True)]
    all_gather x1 -> x0, blocking collectives: 46.1 us -> none  [body(): columns = lax.all_gather(out_weight, 'dp', axis=1, tiled=True)]
    all_to_all x7 -> x0, starting transfers between devices: 33.7 us -> none  [the longest x1 9.09 us: body(): lax.all_to_all(value_saved, 'seq', split_axis=2, concat_axis=1, tiled=True)]
    dot_general x7 -> x0, matrix products: 12.3 us -> none  [the longest x1 4.64 us: body(): jnp.einsum('td,rd->tr', flat_grad, lax.all_gather(columns, 'seq', axis=0,...]
    reshape x11 -> x0, local copies, waits for them, and re-layouts: 7.11 us -> none  [the longest x4 2.13 us: split_heads(): tensor.reshape(tensor.shape[1], tensor.shape[2], tensor.shape[3] // HD, HD)]
    unnamed x10 -> x13, local copies, waits for them, and re-layouts: 11 us -> 7.26 us
  transfers between devices with their start and end apart: 8 -> 0, of which waited for: 7 -> 0; matrix products, arithmetic and copies ran while one was open for 8% -> 0% of each run, Pallas kernels for 0% -> 0%
where the time goes in v1:
time: 125 us
  Pallas kernels  117 us (94%)
  local copies, waits for them, and re-layouts  7.26 us (6%)
    pallas_call x1, Pallas kernels, body(): pl.pallas_call(kernel, out_shape=(shape, shape, shape), in_specs=[anywher...  117 us
    unnamed x13, local copies, waits for them, and re-layouts  7.26 us

profile of v1, /device:TPU:1, one launch (start us, length us, event | category | flops | bytes accessed | tf_op | source)
XLA Modules:
  0.0 124.7 jit_solution(5548771703630978529)
XLA Ops:
  0.6 0.0 copy-start
  0.6 1.0 copy-done
  1.7 0.0 copy-start.1
  1.7 1.0 copy-done.1
  2.7 0.0 copy-start.2
  2.7 1.0 copy-done.2
  3.8 0.0 copy-start.3
  3.8 1.0 copy-done.3
  4.8 0.0 copy-start.4
  4.8 0.7 copy-done.4
  5.5 116.8 %shard_map.76 = (bf16[1,4,32,2048]{3,2,1,0:T(8,128)(2,1)S(1)}, bf16[1,4,32,2048]{3,2,1,0:T(8,128)(2,1)S(1)}, bf16[1,4,32,2048]{3,2,1,0:T(8,128)(2,1)S(1)}) custom-call(bf16[1,4,32,2048]{3,2,1,0:T(8,128)(2,1)S(1)} %copy-done, bf16[1,4,32,2048]{3,2,1,0:T(8,128)(2,1)S(1)} %copy-done.1, bf16[1,4,32,2048]{3,2,1,0:T(8,128)(2,1)S(1)} %copy-done.2, ...), custom_call_target="tpu_custom_call" | custom-call | tf_op jit(solution)/shard_map/pallas_call | solution.py:311
  122.3 0.8 copy.11
  123.1 0.8 copy.12
  123.9 0.8 copy.13
Async XLA Ops:
  0.6 1.0 copy-start
  1.7 1.0 copy-start.1
  2.7 1.0 copy-start.2
  3.8 1.0 copy-start.3
  4.8 0.7 copy-start.4

commit v2 on v1

--- a/solution.py
+++ b/solution.py
@@ -23,12 +23,17 @@
 
 def kernel(
     q, k, v, g, w, oq, ok, ov,
-    rq, rk, rv, rg, gbuf, wt, ga, x32, qt, kt, vt, gt, pt, o32, so,
+    rq, rk, rv, rg, gbuf, wt, acc, ga, x32, qt, kt, vt, gt, pt, o32, so,
     in_send, in_recv, w_send, w_recv, z_send, z_recv, g_send, g_recv, ga_send, ga_recv, o_send, o_recv,
 ):
     dp, s = lax.axis_index("dp"), lax.axis_index("seq")
     z, u = lax.div(dp, 4), lax.rem(dp, 4)
-    own_class = lax.div(s, 4)
+    own_class = lax.rem(s, 2) * 2 + lax.rem(lax.div(s, 2), 2)
+    place = lax.div(s, 4)
+
+    def head(j):
+        return 4 * j + 2 * lax.rem(u, 2) + lax.div(u, 2)
+
     base = z * 4
     own = own_class == u
     inv_root = 1.0 / math.sqrt(HD)
@@ -54,9 +59,9 @@
     def greet_group(i, _):
         t = lax.rem(s + i, 16)
 
-        @pl.when(jnp.logical_or(base + lax.div(t, 4) != dp, 4 * u + lax.rem(t, 4) != s))
+        @pl.when(jnp.logical_or(base + lax.div(t, 4) != dp, head(lax.rem(t, 4)) != s))
         def _():
-            greet(base + lax.div(t, 4), 4 * u + lax.rem(t, 4))
+            greet(base + lax.div(t, 4), head(lax.rem(t, 4)))
 
         @pl.when(jnp.logical_or(own_class != u, t != s))
         def _():
@@ -70,7 +75,7 @@
     pl.semaphore_wait(barrier, 51 - 2 * own.astype(jnp.int32))
 
     def w_rows():
-        return wt.at[pl.ds(pl.multiple_of(dp * 64, 64), 64), pl.ds(pl.multiple_of(lax.rem(s, 4) * HD, HD), HD)]
+        return wt.at[pl.ds(pl.multiple_of(dp * 64, 64), 64), pl.ds(pl.multiple_of(place * HD, HD), HD)]
 
     def w_copy(t):
         return pltpu.make_async_remote_copy(
@@ -141,6 +146,20 @@
     hops = [(step, way, h) for step in range(4) for h in range(2) for way in range(2) if step < 3 or way == h]
     mine = wt.at[pl.ds(pl.multiple_of(z * 256, 256), 256)]
     pltpu.make_async_copy(mine, mine, w_recv).wait()
+
+    def project(slab, first=False):
+        cols = pl.ds(pl.multiple_of(slab * 256, 256), 256)
+
+        def step(half, _):
+            part = dot(
+                gbuf[:, :, :, cols].reshape(512, 256),
+                wt[cols, pl.ds(pl.multiple_of(half * 256, 256), 256)], NN)
+            acc[half] = part if first else acc[half] + part
+            return 0
+
+        lax.fori_loop(0, 2, step, 0)
+
+    ready = [0]
     for step, way, h in hops:
         if step:
             z_arrived(way, h, step - 1)
@@ -148,20 +167,28 @@
         if (step, way, h) == (1, 1, 1):
             to_across.wait_recv()
             onward.start()
+        if (step, way, h) == (2, 0, 0):
+            pltpu.make_async_copy(g.at[0], gbuf.at[u], g_recv.at[0]).wait()
+            to_sibling.wait_recv()
+            onward.wait_recv()
+        if step in (1, 2) and h == 1:
+            ready.append(step if way else -step)
+        if step >= 2 and ready:
+            slab = ready.pop(0)
+            project(ring(z + slab, 8), first=slab == 0)
     for way, h in ((0, 1), (1, 0)):
         z_arrived(way, h, 2)
+    ready += [-3, 3]
+    for slab in ready:
+        project(ring(z + slab, 8))
     for way in range(2):
         z_arrived(way, way, 3)
-
-    pltpu.make_async_copy(g.at[0], gbuf.at[u], g_recv.at[0]).wait()
-    to_sibling.wait_recv()
-    onward.wait_recv()
+    project(ring(z + 4, 8))
 
     for half in range(2):
-        acc = dot(gbuf[...].reshape(512, 2048), wt[:, half * 256 : half * 256 + 256], NN)
-        acc = acc.astype(BF16)
+        val = acc[half].astype(BF16)
         for j in range(2):
-            ga[2 * half + j] = acc[:, j * HD : (j + 1) * HD].reshape(4, 4, 32, HD)
+            ga[2 * half + j] = val[:, j * HD : (j + 1) * HD].reshape(4, 4, 32, HD)
 
     def patches(c):
         return pl.ds(c * 16, 16)
@@ -171,14 +198,14 @@
         return pltpu.make_async_remote_copy(
             src_ref=ga.at[j, b, :, patches(c)], dst_ref=rg.at[s, :, patches(c)],
             send_sem=ga_send.at[c], recv_sem=ga_recv.at[c],
-            device_id=(base + b, 4 * u + j), device_id_type=MESH)
+            device_id=(base + b, head(j)), device_id_type=MESH)
 
     for c in range(2):
 
         def ga_go(i, _, c=c):
             t = lax.rem(s + i, 16)
             b, j = lax.div(t, 4), lax.rem(t, 4)
-            mine = jnp.logical_and(b == u, 4 * u + j == s)
+            mine = jnp.logical_and(b == u, head(j) == s)
 
             @pl.when(mine)
             def _():
@@ -317,6 +344,7 @@
             *[pltpu.VMEM((16, 4, 32, HD), BF16)] * 4,
             pltpu.VMEM((4, 4, 32, 2048), BF16),
             pltpu.VMEM((2048, 512), BF16),
+            pltpu.VMEM((2, 512, 256), F32),
             pltpu.VMEM((4, 4, 4, 32, HD), BF16),
             pltpu.VMEM((2048, HD), F32),
             *[pltpu.VMEM((16, 128, HD), BF16)] * 4,
@@ -331,7 +359,7 @@
             dma((3,)), dma((3,)),
         ],
         compiler_params=pltpu.CompilerParams(
-            collective_id=0, has_side_effects=True, vmem_limit_bytes=48 * 1024 * 1024),
+            collective_id=0, has_side_effects=True, vmem_limit_bytes=60 * 1024 * 1024),
     )(query_saved, key_saved, value_saved, grad_block, out_weight.T)
 
 

time: 125 us -> 110 us (0.88)
  Pallas kernels: 117 us -> 105 us
  local copies, waits for them, and re-layouts: 7.26 us -> 3.97 us
    pallas_call x1, Pallas kernels: 117 us -> 105 us  [body(): pl.pallas_call(kernel, out_shape=(shape, shape, shape), in_specs=[anywher...]
    unnamed x13 -> x7, local copies, waits for them, and re-layouts: 7.26 us -> 3.97 us
where the time goes in v2:
time: 110 us; the launch traced here: 109 us
  Pallas kernels  105 us (95%)
  local copies, waits for them, and re-layouts  3.97 us (4%)
    pallas_call x1, Pallas kernels, body(): pl.pallas_call(kernel, out_shape=(shape, shape, shape), in_specs=[anywher...  105 us
    unnamed x7, local copies, waits for them, and re-layouts  3.97 us

profile of v2, /device:TPU:1, one launch (start us, length us, event | category | flops | bytes accessed | tf_op | source)
XLA Modules:
  0.0 109.3 jit_solution(4788122288954492835)
XLA Ops:
  0.6 104.7 %shard_map.76 = (bf16[1,4,32,2048]{3,2,1,0:T(8,128)(2,1)}, bf16[1,4,32,2048]{3,2,1,0:T(8,128)(2,1)}, bf16[1,4,32,2048]{3,2,1,0:T(8,128)(2,1)}) custom-call(bf16[1,4,32,2048]{3,2,1,0:T(8,128)(2,1)} %q.1, bf16[1,4,32,2048]{3,2,1,0:T(8,128)(2,1)} %k.1, bf16[1,4,32,2048]{3,2,1,0:T(8,128)(2,1)} %v.1, bf16[1,4,32,2048]{3,2,1,0:T(8,128)(2,1)} %g.1, ...), custom_call_target="tpu_custom_call" | custom-call | tf_op jit(solution)/shard_map/pallas_call | solution.py:338
  105.4 0.0 copy-start.1
  105.4 1.9 %copy.11 = bf16[1,4,32,2048]{3,2,1,0:T(8,128)(2,1)} copy(bf16[1,4,32,2048]{3,2,1,0:T(8,128)(2,1)} %get-tuple-element.6) | data formatting | bytes 1048576
  107.3 0.0 copy-done.1
  107.3 0.0 copy-start
  107.3 0.8 copy.12
  108.1 0.4 copy-done
  108.5 0.8 copy.13
Async XLA Ops:
  105.4 2.0 %copy-start.1 = (bf16[1,4,32,2048]{3,2,1,0:T(8,128)(2,1)S(1)}, bf16[1,4,32,2048]{3,2,1,0:T(8,128)(2,1)}, u32[]{:S(2)}) copy-start(bf16[1,4,32,2048]{3,2,1,0:T(8,128)(2,1)} %get-tuple-element.7) | copy-start | bytes 1572868
  107.3 1.2 %copy-start = (bf16[1,4,32,2048]{3,2,1,0:T(8,128)(2,1)S(1)}, bf16[1,4,32,2048]{3,2,1,0:T(8,128)(2,1)}, u32[]{:S(2)}) copy-start(bf16[1,4,32,2048]{3,2,1,0:T(8,128)(2,1)} %get-tuple-element.8) | copy-start | bytes 1572868

commit v3 on v2

--- a/solution.py
+++ b/solution.py
@@ -331,13 +331,22 @@
         drain(outs[n], o_recv.at[n])
 
 
+def put(a, b, c, oa, ob, oc, sem):
+    copies = [pltpu.make_async_copy(src, dst, sem.at[n]) for n, (src, dst) in enumerate(((a, oa), (b, ob), (c, oc)))]
+    for copy in copies:
+        copy.start()
+    for copy in copies:
+        copy.wait()
+
+
 def body(query_saved, key_saved, value_saved, grad_block, out_weight):
     shape = jax.ShapeDtypeStruct(query_saved.shape, BF16)
     anywhere = pl.BlockSpec(memory_space=pl.ANY)
     dma = pltpu.SemaphoreType.DMA
-    return pl.pallas_call(
+    near = pltpu.VMEM(query_saved.shape, BF16)
+    grads = pl.pallas_call(
         kernel,
-        out_shape=(shape, shape, shape),
+        out_shape=(near, near, near),
         in_specs=[anywhere] * 5,
         out_specs=(anywhere,) * 3,
         scratch_shapes=[
@@ -361,6 +370,10 @@
         compiler_params=pltpu.CompilerParams(
             collective_id=0, has_side_effects=True, vmem_limit_bytes=60 * 1024 * 1024),
     )(query_saved, key_saved, value_saved, grad_block, out_weight.T)
+    return pl.pallas_call(
+        put, out_shape=(shape, shape, shape), in_specs=[pl.BlockSpec(memory_space=pltpu.VMEM)] * 3,
+        out_specs=(anywhere,) * 3, scratch_shapes=[dma((3,))],
+    )(*[pltpu.with_memory_space_constraint(a, pltpu.VMEM) for a in grads])
 
 
 def solution(mesh):

time: 110 us -> 107 us (0.973)
  local copies, waits for them, and re-layouts: 3.97 us -> 0 us
    unnamed x7 -> x0, local copies, waits for them, and re-layouts: 3.97 us -> none
    pallas_call x1 -> x2, Pallas kernels: 105 us -> 106 us  [the longest x1 105 us: body(): pl.pallas_call(kernel, out_shape=(near, near, near), in_specs=[anywhere]...]
where the time goes in v3:
time: 107 us; the launch traced here: 106 us
  Pallas kernels  106 us (99%)
    pallas_call x1, Pallas kernels, body(): pl.pallas_call(kernel, out_shape=(near, near, near), in_specs=[anywhere]...  105 us

profile of v3, /device:TPU:1, one launch (start us, length us, event | category | flops | bytes accessed | tf_op | source)
XLA Modules:
  0.0 106.4 jit_solution(9672478211661109488)
XLA Ops:
  0.6 104.6 %shard_map.76 = (bf16[1,4,32,2048]{3,2,1,0:T(8,128)(2,1)S(1)}, bf16[1,4,32,2048]{3,2,1,0:T(8,128)(2,1)S(1)}, bf16[1,4,32,2048]{3,2,1,0:T(8,128)(2,1)S(1)}) custom-call(bf16[1,4,32,2048]{3,2,1,0:T(8,128)(2,1)} %q.1, bf16[1,4,32,2048]{3,2,1,0:T(8,128)(2,1)} %k.1, bf16[1,4,32,2048]{3,2,1,0:T(8,128)(2,1)} %v.1, bf16[1,4,32,2048]{3,2,1,0:T(8,128)(2,1)} %g.1, ...), custom_call_target="tpu_custom_call" | custom-call | tf_op jit(solution)/shard_map/pallas_call | solution.py:347
  105.2 1.2 %shard_map.77 = (bf16[1,4,32,2048]{3,2,1,0:T(8,128)(2,1)}, bf16[1,4,32,2048]{3,2,1,0:T(8,128)(2,1)}, bf16[1,4,32,2048]{3,2,1,0:T(8,128)(2,1)}) custom-call(bf16[1,4,32,2048]{3,2,1,0:T(8,128)(2,1)S(1)} %get-tuple-element.6.a, bf16[1,4,32,2048]{3,2,1,0:T(8,128)(2,1)S(1)} %get-tuple-element.7.b, bf16[1,4,32,2048]{3,2,1,0:T(8,128)(2,1)S(1)} %get-tuple-element.8.c), custom_call_target="tpu_custom_call" | custom-call | tf_op jit(solution)/shard_map/pallas_call | solution.py:373

commit v4 on v1

--- a/solution.py
+++ b/solution.py
@@ -11,6 +11,7 @@
 HD = 128
 F32 = jnp.float32
 BF16 = jnp.bfloat16
+HOP = (0, 1, 1)
 MESH = pl.DeviceIdType.MESH
 NT = (((1,), (1,)), ((), ()))
 TN = (((0,), (0,)), ((), ()))
@@ -28,17 +29,28 @@
 ):
     dp, s = lax.axis_index("dp"), lax.axis_index("seq")
     z, u = lax.div(dp, 4), lax.rem(dp, 4)
-    own_class = lax.div(s, 4)
+    y, xh = lax.div(s, 2), lax.rem(s, 2)
+    x, core = 2 * xh + lax.div(u, 2), lax.rem(u, 2)
     base = z * 4
-    own = own_class == u
+    own = u == 0
     inv_root = 1.0 / math.sqrt(HD)
 
     def ring(i, n):
         return lax.rem(i + n, n)
 
+    def on_x(at):
+        return base + 2 * lax.rem(at, 2) + core, y * 2 + lax.div(at, 2)
+
+    def head(j):
+        return lax.rem(y + 4 * core + 2 * j + lax.div(u, 2), 8) * 2 + xh
+
+    def holder(at):
+        o = ring(y - at, 8)
+        return base + 2 * lax.rem(o, 2) + lax.div(o, 4), at * 2 + xh
+
     up, down = ring(z + 1, 8) * 4 + u, ring(z - 1, 8) * 4 + u
-    sibling = base + (u + 1 - 2 * lax.rem(u, 2))
-    across = base + lax.rem(u + 2, 4)
+    sibling = base + u + 1 - 2 * core
+    right, left = on_x(ring(x + 1, 4)), on_x(ring(x - 1, 4))
 
     barrier = pltpu.get_barrier_semaphore()
 
@@ -51,78 +63,95 @@
 
     lax.fori_loop(1, 16, greet_seq, 0)
 
+    def other(d, e):
+        return jnp.logical_or(d != dp, e != s)
+
     def greet_group(i, _):
-        t = lax.rem(s + i, 16)
-
-        @pl.when(jnp.logical_or(base + lax.div(t, 4) != dp, 4 * u + lax.rem(t, 4) != s))
+        d, e = holder(i)
+
+        @pl.when(other(d, e))
         def _():
-            greet(base + lax.div(t, 4), 4 * u + lax.rem(t, 4))
-
-        @pl.when(jnp.logical_or(own_class != u, t != s))
+            greet(d, e)
+
+        d, e = base + lax.rem(i, 4), head(lax.div(i, 4))
+
+        @pl.when(other(d, e))
         def _():
-            greet(base + own_class, t)
+            greet(d, e)
 
         return 0
 
-    lax.fori_loop(0, 16, greet_group, 0)
-    for d in (up, down, sibling, across):
-        greet(d, s)
-    pl.semaphore_wait(barrier, 51 - 2 * own.astype(jnp.int32))
-
-    def w_rows():
-        return wt.at[pl.ds(pl.multiple_of(dp * 64, 64), 64), pl.ds(pl.multiple_of(lax.rem(s, 4) * HD, HD), HD)]
-
-    def w_copy(t):
+    lax.fori_loop(0, 8, greet_group, 0)
+    for d, e in ((up, s), (down, s), (sibling, s), left, right):
+        greet(d, e)
+    pl.semaphore_wait(barrier, 36 - 2 * own.astype(jnp.int32))
+
+    def w_rows(at):
+        j = lax.rem(lax.div(ring(y - at, 8), 2), 2)
+        return wt.at[pl.ds(pl.multiple_of(dp * 64, 64), 64), pl.ds(pl.multiple_of(j * HD, HD), HD)]
+
+    def w_go(i, _):
+        at = lax.rem(y + i, 8)
+        d, e = holder(at)
+
+        @pl.when(other(d, e))
+        def _():
+            pltpu.make_async_remote_copy(
+                src_ref=w, dst_ref=w_rows(at), send_sem=w_send, recv_sem=w_recv,
+                device_id=(d, e), device_id_type=MESH).start()
+
+        @pl.when(jnp.logical_not(other(d, e)))
+        def _():
+            pltpu.make_async_copy(w, w_rows(at), w_recv).start()
+
+        return 0
+
+    lax.fori_loop(0, 8, w_go, 0)
+
+    def block(at, c):
+        return gbuf.at[2 * at + c]
+
+    def g_copy(n, src, dst, to):
         return pltpu.make_async_remote_copy(
-            src_ref=w, dst_ref=w_rows(), send_sem=w_send, recv_sem=w_recv,
-            device_id=(base + own_class, t), device_id_type=MESH)
-
-    def w_go(i, _):
-        t = lax.rem(s + i, 16)
-        mine = jnp.logical_and(own, t == s)
-
-        @pl.when(mine)
-        def _():
-            pltpu.make_async_copy(w, w_rows(), w_recv).start()
-
-        @pl.when(jnp.logical_not(mine))
-        def _():
-            w_copy(t).start()
-
-        return 0
-
-    lax.fori_loop(0, 16, w_go, 0)
-
-    pltpu.make_async_copy(g.at[0], gbuf.at[u], g_recv.at[0]).start()
-
-    def g_copy(n, src, slot, d):
-        return pltpu.make_async_remote_copy(
-            src_ref=src, dst_ref=gbuf.at[slot], send_sem=g_send.at[n], recv_sem=g_recv.at[n],
-            device_id=(d, s), device_id_type=MESH)
-
-    to_across = g_copy(1, g.at[0], u, across)
-    to_sibling = g_copy(2, g.at[0], u, sibling)
-    across_slot = lax.rem(u + 2, 4)
-    onward = g_copy(3, gbuf.at[across_slot], across_slot, sibling)
-    to_across.start()
-    to_sibling.start()
+            src_ref=src, dst_ref=dst, send_sem=g_send.at[n], recv_sem=g_recv.at[n],
+            device_id=to, device_id_type=MESH)
+
+    twin = (sibling, s)
+    mine, before, after, across = (block(ring(x + i, 4), core) for i in (0, -1, 1, 2))
+    near, far = pl.ds(0, 2), pl.ds(2, 2)
+    g_own = pltpu.make_async_copy(g.at[0], mine, g_recv.at[0])
+    to_right = g_copy(1, g.at[0], mine, right)
+    to_left = g_copy(2, g.at[0], mine, left)
+    to_twin = g_copy(3, g.at[0], mine, twin)
+    on_right = g_copy(4, before.at[near], before.at[near], right)
+    on_left = g_copy(5, after.at[far], after.at[far], left)
+    twin_before = g_copy(6, before, before, twin)
+    twin_after = g_copy(7, after, after, twin)
+    twin_near = g_copy(8, across.at[near], across.at[near], twin)
+    twin_far = g_copy(9, across.at[far], across.at[far], twin)
+    for copy in (g_own, to_right, to_left, to_twin):
+        copy.start()
 
     pairs = ((q, rq), (k, rk), (v, rv))
 
     def lanes(h):
         return pl.ds(pl.multiple_of(h * HD, HD), HD)
 
+    def send_in(flip):
+        for n, (src, dst) in enumerate(pairs):
+
+            def in_go(i, _, src=src, dst=dst, n=n):
+                t = lax.rem(y + i, 8) * 2 + (1 - xh if flip else xh)
+                pltpu.make_async_remote_copy(
+                    src_ref=src.at[0, :, :, lanes(t)], dst_ref=dst.at[s], send_sem=in_send.at[n], recv_sem=in_recv.at[n],
+                    device_id=(dp, t), device_id_type=MESH).start()
+                return 0
+
+            lax.fori_loop(0 if flip else 1, 8, in_go, 0)
+
     for n, (src, dst) in enumerate(pairs):
         pltpu.make_async_copy(src.at[0, :, :, lanes(s)], dst.at[s], in_recv.at[n]).start()
-
-        def in_go(i, _, src=src, dst=dst, n=n):
-            t = lax.rem(s + i, 16)
-            pltpu.make_async_remote_copy(
-                src_ref=src.at[0, :, :, lanes(t)], dst_ref=dst.at[s], send_sem=in_send.at[n], recv_sem=in_recv.at[n],
-                device_id=(dp, t), device_id_type=MESH).start()
-            return 0
-
-        lax.fori_loop(1, 16, in_go, 0)
+    send_in(False)
 
     def z_copy(way, h, step):
         slab = ring(z - step, 8) if way == 0 else ring(z + step, 8)
@@ -139,54 +168,62 @@
             device_id=(up if way == 0 else down, s), device_id_type=MESH).wait_recv()
 
     hops = [(step, way, h) for step in range(4) for h in range(2) for way in range(2) if step < 3 or way == h]
-    mine = wt.at[pl.ds(pl.multiple_of(z * 256, 256), 256)]
-    pltpu.make_async_copy(mine, mine, w_recv).wait()
+    slab = wt.at[pl.ds(pl.multiple_of(z * 256, 256), 256)]
+    pltpu.make_async_copy(slab, slab, w_recv).wait()
+
+    def first_hop():
+        to_right.wait_recv()
+        on_right.start()
+        twin_before.start()
+        to_left.wait_recv()
+        on_left.start()
+        twin_after.start()
+        send_in(True)
+
     for step, way, h in hops:
         if step:
             z_arrived(way, h, step - 1)
         z_copy(way, h, step).start()
-        if (step, way, h) == (1, 1, 1):
-            to_across.wait_recv()
-            onward.start()
+        if (step, way, h) == HOP:
+            first_hop()
+    on_right.wait_recv()
+    twin_near.start()
+    on_left.wait_recv()
+    twin_far.start()
     for way, h in ((0, 1), (1, 0)):
         z_arrived(way, h, 2)
     for way in range(2):
         z_arrived(way, way, 3)
-
-    pltpu.make_async_copy(g.at[0], gbuf.at[u], g_recv.at[0]).wait()
-    to_sibling.wait_recv()
-    onward.wait_recv()
+    g_own.wait()
+    for copy in (to_twin, twin_before, twin_after, twin_near, twin_far):
+        copy.wait_recv()
 
     for half in range(2):
-        acc = dot(gbuf[...].reshape(512, 2048), wt[:, half * 256 : half * 256 + 256], NN)
-        acc = acc.astype(BF16)
+        val = dot(gbuf[4 * half : 4 * half + 4].reshape(512, 2048), wt[...], NN).astype(BF16)
         for j in range(2):
-            ga[2 * half + j] = acc[:, j * HD : (j + 1) * HD].reshape(4, 4, 32, HD)
+            ga[j, 4 * half : 4 * half + 4] = val[:, j * HD : (j + 1) * HD].reshape(4, 4, 32, HD)
 
     def patches(c):
         return pl.ds(c * 16, 16)
 
-    def ga_copy(c, t):
-        b, j = lax.div(t, 4), lax.rem(t, 4)
-        return pltpu.make_async_remote_copy(
-            src_ref=ga.at[j, b, :, patches(c)], dst_ref=rg.at[s, :, patches(c)],
-            send_sem=ga_send.at[c], recv_sem=ga_recv.at[c],
-            device_id=(base + b, 4 * u + j), device_id_type=MESH)
-
     for c in range(2):
 
         def ga_go(i, _, c=c):
             t = lax.rem(s + i, 16)
-            b, j = lax.div(t, 4), lax.rem(t, 4)
-            mine = jnp.logical_and(b == u, 4 * u + j == s)
-
-            @pl.when(mine)
+            b, j = lax.rem(t, 8), lax.div(t, 8)
+            at = lax.div(b, 2)
+            d, e = base + 2 * lax.rem(at, 2) + lax.rem(b, 2), head(j)
+            src, dst = ga.at[j, b, :, patches(c)], rg.at[2 * y + lax.div(at, 2), :, patches(c)]
+
+            @pl.when(other(d, e))
             def _():
-                pltpu.make_async_copy(ga.at[j, b, :, patches(c)], rg.at[s, :, patches(c)], ga_recv.at[c]).start()
-
-            @pl.when(jnp.logical_not(mine))
+                pltpu.make_async_remote_copy(
+                    src_ref=src, dst_ref=dst, send_sem=ga_send.at[c], recv_sem=ga_recv.at[c],
+                    device_id=(d, e), device_id_type=MESH).start()
+
+            @pl.when(jnp.logical_not(other(d, e)))
             def _():
-                ga_copy(c, t).start()
+                pltpu.make_async_copy(src, dst, ga_recv.at[c]).start()
 
             return 0
 
@@ -281,7 +318,7 @@
         pltpu.make_async_copy(part, part, in_send.at[n]).wait()
     for step, way, h in hops:
         z_copy(way, h, step).wait_send()
-    for copy in (to_across, to_sibling, onward):
+    for copy in (to_right, to_left, to_twin, on_right, on_left, twin_before, twin_after, twin_near, twin_far):
         copy.wait_send()
 
     def drain(ref, sem):
@@ -289,9 +326,9 @@
 
     @pl.when(own)
     def _():
-        drain(wt.at[pl.ds(0, 240)], w_send)
+        drain(wt.at[pl.ds(0, 224)], w_send)
         for c in range(2):
-            drain(rg.at[pl.ds(0, 15), :, patches(c)], ga_send.at[c])
+            drain(rg.at[pl.ds(0, 14), :, patches(c)], ga_send.at[c])
 
     @pl.when(jnp.logical_not(own))
     def _():
@@ -304,20 +341,29 @@
         drain(outs[n], o_recv.at[n])
 
 
+def put(a, b, c, oa, ob, oc, sem):
+    copies = [pltpu.make_async_copy(src, dst, sem.at[n]) for n, (src, dst) in enumerate(((a, oa), (b, ob), (c, oc)))]
+    for copy in copies:
+        copy.start()
+    for copy in copies:
+        copy.wait()
+
+
 def body(query_saved, key_saved, value_saved, grad_block, out_weight):
     shape = jax.ShapeDtypeStruct(query_saved.shape, BF16)
     anywhere = pl.BlockSpec(memory_space=pl.ANY)
     dma = pltpu.SemaphoreType.DMA
-    return pl.pallas_call(
+    near = pltpu.VMEM(query_saved.shape, BF16)
+    grads = pl.pallas_call(
         kernel,
-        out_shape=(shape, shape, shape),
+        out_shape=(near, near, near),
         in_specs=[anywhere] * 5,
         out_specs=(anywhere,) * 3,
         scratch_shapes=[
             *[pltpu.VMEM((16, 4, 32, HD), BF16)] * 4,
-            pltpu.VMEM((4, 4, 32, 2048), BF16),
-            pltpu.VMEM((2048, 512), BF16),
-            pltpu.VMEM((4, 4, 4, 32, HD), BF16),
+            pltpu.VMEM((8, 4, 32, 2048), BF16),
+            pltpu.VMEM((2048, 256), BF16),
+            pltpu.VMEM((2, 8, 4, 32, HD), BF16),
             pltpu.VMEM((2048, HD), F32),
             *[pltpu.VMEM((16, 128, HD), BF16)] * 4,
             pltpu.VMEM((16, 128, 128), F32),
@@ -326,13 +372,17 @@
             dma((3,)), dma((3,)),
             dma, dma,
             dma((2, 2, 4)), dma((2, 2, 4)),
-            dma((4,)), dma((4,)),
+            dma((10,)), dma((10,)),
             dma((2,)), dma((2,)),
             dma((3,)), dma((3,)),
         ],
         compiler_params=pltpu.CompilerParams(
-            collective_id=0, has_side_effects=True, vmem_limit_bytes=48 * 1024 * 1024),
+            collective_id=0, has_side_effects=True, vmem_limit_bytes=60 * 1024 * 1024),
     )(query_saved, key_saved, value_saved, grad_block, out_weight.T)
+    return pl.pallas_call(
+        put, out_shape=(shape, shape, shape), in_specs=[pl.BlockSpec(memory_space=pltpu.VMEM)] * 3,
+        out_specs=(anywhere,) * 3, scratch_shapes=[dma((3,))],
+    )(*[pltpu.with_memory_space_constraint(a, pltpu.VMEM) for a in grads])
 
 
 def solution(mesh):

time: 125 us -> 104 us (0.83)
  Pallas kernels: 117 us -> 103 us
  local copies, waits for them, and re-layouts: 7.26 us -> 0 us
    pallas_call x1 -> x2, Pallas kernels: 117 us -> 103 us  [the longest x1 101 us: body(): pl.pallas_call(kernel, out_shape=(near, near, near), in_specs=[anywhere]...]
    unnamed x13 -> x0, local copies, waits for them, and re-layouts: 7.26 us -> none
where the time goes in v4:
time: 104 us; the launch traced here: 103 us
  Pallas kernels  103 us (99%)
    pallas_call x1, Pallas kernels, body(): pl.pallas_call(kernel, out_shape=(near, near, near), in_specs=[anywhere]...  101 us

profile of v4, /device:TPU:1, one launch (start us, length us, event | category | flops | bytes accessed | tf_op | source)
XLA Modules:
  0.0 103.2 jit_solution(5524354090598601791)
XLA Ops:
  0.6 101.4 %shard_map.76 = (bf16[1,4,32,2048]{3,2,1,0:T(8,128)(2,1)S(1)}, bf16[1,4,32,2048]{3,2,1,0:T(8,128)(2,1)S(1)}, bf16[1,4,32,2048]{3,2,1,0:T(8,128)(2,1)S(1)}) custom-call(bf16[1,4,32,2048]{3,2,1,0:T(8,128)(2,1)} %q.1, bf16[1,4,32,2048]{3,2,1,0:T(8,128)(2,1)} %k.1, bf16[1,4,32,2048]{3,2,1,0:T(8,128)(2,1)} %v.1, bf16[1,4,32,2048]{3,2,1,0:T(8,128)(2,1)} %g.1, ...), custom_call_target="tpu_custom_call" | custom-call | tf_op jit(solution)/shard_map/pallas_call | solution.py:357
  102.0 1.2 %shard_map.77 = (bf16[1,4,32,2048]{3,2,1,0:T(8,128)(2,1)}, bf16[1,4,32,2048]{3,2,1,0:T(8,128)(2,1)}, bf16[1,4,32,2048]{3,2,1,0:T(8,128)(2,1)}) custom-call(bf16[1,4,32,2048]{3,2,1,0:T(8,128)(2,1)S(1)} %get-tuple-element.6.a, bf16[1,4,32,2048]{3,2,1,0:T(8,128)(2,1)S(1)} %get-tuple-element.7.b, bf16[1,4,32,2048]{3,2,1,0:T(8,128)(2,1)S(1)} %get-tuple-element.8.c), custom_call_target="tpu_custom_call" | custom-call | tf_op jit(solution)/shard_map/pallas_call | solution.py:382

commit v5 on v4

--- a/solution.py
+++ b/solution.py
@@ -282,22 +282,26 @@
 
         lax.fori_loop(0, 16, widen_g, 0)
 
-        def grads(p, _):
-            gp, vp, prob = pair_of(p), vt[p], pt[p]
-            low = prob.astype(BF16)
-            grad_prob = dot(vp, gp, NT)
-            delta = jnp.sum(low.astype(F32) * grad_prob, axis=0, keepdims=True)
+        def value_grad(p, _):
+            gp = pair_of(p)
+            gt[p] = gp
+            val = dot(pt[p].astype(BF16), gp, NN)
+            o32[2, pl.ds(2 * p, 64, stride=32), :] = val[:64]
+            o32[2, pl.ds(2 * p + 1, 64, stride=32), :] = val[64:]
+            return 0
+
+        def score_grads(p, _):
+            prob = pt[p]
+            grad_prob = dot(vt[p], gt[p], NT)
+            delta = jnp.sum(prob.astype(BF16).astype(F32) * grad_prob, axis=0, keepdims=True)
             ds = (prob * (grad_prob - delta) * inv_root).astype(BF16)
-            for n, val in ((2, dot(low, gp, NN)), (1, dot(ds, qt[p], NN)), (0, dot(ds, kt[p], TN))):
+            for n, val in ((1, dot(ds, qt[p], NN)), (0, dot(ds, kt[p], TN))):
                 o32[n, pl.ds(2 * p, 64, stride=32), :] = val[:64]
                 o32[n, pl.ds(2 * p + 1, 64, stride=32), :] = val[64:]
             return 0
 
-        lax.fori_loop(c * 8, c * 8 + 8, grads, 0)
-
-        for n in range(3):
-
-            def narrow(i, _, n=n, c=c):
+        def give(n, c=c):
+            def narrow(i, _):
                 for f in range(4):
                     rows = pl.ds(pl.multiple_of(i * 128 + f * 32 + c * 16, 16), 16)
                     so[n, i, f, c * 16 : c * 16 + 16] = o32[n, rows, :].astype(BF16)
@@ -307,11 +311,17 @@
             pltpu.make_async_copy(
                 so.at[n, s, :, patches(c)], outs[n].at[0, :, patches(c), lanes(s)], o_recv.at[n]).start()
 
-            def out_go(i, _, n=n, c=c):
+            def out_go(i, _):
                 out_copy(n, c, lax.rem(s + i, 16)).start()
                 return 0
 
             lax.fori_loop(1, 16, out_go, 0)
+
+        lax.fori_loop(c * 8, c * 8 + 8, value_grad, 0)
+        give(2)
+        lax.fori_loop(c * 8, c * 8 + 8, score_grads, 0)
+        give(1)
+        give(0)
 
     for n, (src, dst) in enumerate(pairs):
         part = src.at[0, :, :, pl.ds(0, 15 * HD)]

time: 104 us -> 102 us (0.981)
  Pallas kernels: 103 us -> 99.8 us
    pallas_call x1, Pallas kernels: 101 us -> 98.7 us  [body(): pl.pallas_call(kernel, out_shape=(near, near, near), in_specs=[anywhere]...]
where the time goes in v5:
time: 102 us; the launch traced here: 100 us
  Pallas kernels  99.8 us (98%)
    pallas_call x1, Pallas kernels, body(): pl.pallas_call(kernel, out_shape=(near, near, near), in_specs=[anywhere]...  98.7 us

profile of v5, /device:TPU:1, one launch (start us, length us, event | category | flops | bytes accessed | tf_op | source)
XLA Modules:
  0.0 100.5 jit_solution(7993423099686287127)
XLA Ops:
  0.6 98.7 %shard_map.76 = (bf16[1,4,32,2048]{3,2,1,0:T(8,128)(2,1)S(1)}, bf16[1,4,32,2048]{3,2,1,0:T(8,128)(2,1)S(1)}, bf16[1,4,32,2048]{3,2,1,0:T(8,128)(2,1)S(1)}) custom-call(bf16[1,4,32,2048]{3,2,1,0:T(8,128)(2,1)} %q.1, bf16[1,4,32,2048]{3,2,1,0:T(8,128)(2,1)} %k.1, bf16[1,4,32,2048]{3,2,1,0:T(8,128)(2,1)} %v.1, bf16[1,4,32,2048]{3,2,1,0:T(8,128)(2,1)} %g.1, ...), custom_call_target="tpu_custom_call" | custom-call | tf_op jit(solution)/shard_map/pallas_call | solution.py:367
  99.3 1.2 %shard_map.77 = (bf16[1,4,32,2048]{3,2,1,0:T(8,128)(2,1)}, bf16[1,4,32,2048]{3,2,1,0:T(8,128)(2,1)}, bf16[1,4,32,2048]{3,2,1,0:T(8,128)(2,1)}) custom-call(bf16[1,4,32,2048]{3,2,1,0:T(8,128)(2,1)S(1)} %get-tuple-element.6.a, bf16[1,4,32,2048]{3,2,1,0:T(8,128)(2,1)S(1)} %get-tuple-element.7.b, bf16[1,4,32,2048]{3,2,1,0:T(8,128)(2,1)S(1)} %get-tuple-element.8.c), custom_call_target="tpu_custom_call" | custom-call | tf_op jit(solution)/shard_map/pallas_call | solution.py:392

commit v6 on v5

--- a/solution.py
+++ b/solution.py
@@ -282,12 +282,14 @@
 
         lax.fori_loop(0, 16, widen_g, 0)
 
+        def place(n, p, val):
+            o32[n, pl.ds(2 * p, 64, stride=32), :] = val[:64]
+            o32[n, pl.ds(2 * p + 1, 64, stride=32), :] = val[64:]
+
         def value_grad(p, _):
             gp = pair_of(p)
             gt[p] = gp
-            val = dot(pt[p].astype(BF16), gp, NN)
-            o32[2, pl.ds(2 * p, 64, stride=32), :] = val[:64]
-            o32[2, pl.ds(2 * p + 1, 64, stride=32), :] = val[64:]
+            place(2, p, dot(pt[p].astype(BF16), gp, NN))
             return 0
 
         def score_grads(p, _):
@@ -295,9 +297,12 @@
             grad_prob = dot(vt[p], gt[p], NT)
             delta = jnp.sum(prob.astype(BF16).astype(F32) * grad_prob, axis=0, keepdims=True)
             ds = (prob * (grad_prob - delta) * inv_root).astype(BF16)
-            for n, val in ((1, dot(ds, qt[p], NN)), (0, dot(ds, kt[p], TN))):
-                o32[n, pl.ds(2 * p, 64, stride=32), :] = val[:64]
-                o32[n, pl.ds(2 * p + 1, 64, stride=32), :] = val[64:]
+            vt[p] = ds
+            place(1, p, dot(ds, qt[p], NN))
+            return 0
+
+        def query_grad(p, _):
+            place(0, p, dot(vt[p], kt[p], TN))
             return 0
 
         def give(n, c=c):
@@ -321,6 +326,7 @@
         give(2)
         lax.fori_loop(c * 8, c * 8 + 8, score_grads, 0)
         give(1)
+        lax.fori_loop(c * 8, c * 8 + 8, query_grad, 0)
         give(0)
 
     for n, (src, dst) in enumerate(pairs):

time: 102 us -> 102 us (level)
  no operation moved by 1% of the time
where the time goes in v6:
time: 102 us; the launch traced here: 100 us
  Pallas kernels  99.7 us (98%)
    pallas_call x1, Pallas kernels, body(): pl.pallas_call(kernel, out_shape=(near, near, near), in_specs=[anywhere]...  98.5 us

profile of v6, /device:TPU:1, one launch (start us, length us, event | category | flops | bytes accessed | tf_op | source)
XLA Modules:
  0.0 100.3 jit_solution(12207937885548377615)
XLA Ops:
  0.6 98.5 %shard_map.76 = (bf16[1,4,32,2048]{3,2,1,0:T(8,128)(2,1)S(1)}, bf16[1,4,32,2048]{3,2,1,0:T(8,128)(2,1)S(1)}, bf16[1,4,32,2048]{3,2,1,0:T(8,128)(2,1)S(1)}) custom-call(bf16[1,4,32,2048]{3,2,1,0:T(8,128)(2,1)} %q.1, bf16[1,4,32,2048]{3,2,1,0:T(8,128)(2,1)} %k.1, bf16[1,4,32,2048]{3,2,1,0:T(8,128)(2,1)} %v.1, bf16[1,4,32,2048]{3,2,1,0:T(8,128)(2,1)} %g.1, ...), custom_call_target="tpu_custom_call" | custom-call | tf_op jit(solution)/shard_map/pallas_call | solution.py:373
  99.1 1.2 %shard_map.77 = (bf16[1,4,32,2048]{3,2,1,0:T(8,128)(2,1)}, bf16[1,4,32,2048]{3,2,1,0:T(8,128)(2,1)}, bf16[1,4,32,2048]{3,2,1,0:T(8,128)(2,1)}) custom-call(bf16[1,4,32,2048]{3,2,1,0:T(8,128)(2,1)S(1)} %get-tuple-element.6.a, bf16[1,4,32,2048]{3,2,1,0:T(8,128)(2,1)S(1)} %get-tuple-element.7.b, bf16[1,4,32,2048]{3,2,1,0:T(8,128)(2,1)S(1)} %get-tuple-element.8.c), custom_call_target="tpu_custom_call" | custom-call | tf_op jit(solution)/shard_map/pallas_call | solution.py:398
